TPU v7x, 512 devices: a whole 4x4x16 slice. The times are simulated.
512 devices in a mesh: group: 8 (over x, core), ctx: 64 (over y, z).
Axes of the slice: x: 4, y: 4, z: 16, core: 2. Of those that a mesh axis runs over, the one named last changes fastest.
Arguments:
- projected_queries: bfloat16 [65536, 4096], P(('group', 'ctx')), may hold values from -6 to 6
- projected_keys: bfloat16 [65536, 4096], P(('group', 'ctx')), may hold values from -6 to 6
- projected_values: bfloat16 [65536, 4096], P(('group', 'ctx')), may hold values from -6 to 6
- short_filter_taps: float32 [3, 3, 4096], P(None, None, 'ctx'), may hold values from -3.5 to 3.5
- long_filter_taps: bfloat16 [128, 4096], P(None, 'ctx'), may hold values from -0.5 to 0.5
- adapter_down_weight: bfloat16 [256, 16, 4096], P('ctx', None, 'group'), may hold values from -0.09375 to 0.09375
- adapter_up_weight: bfloat16 [256, 16, 4096], P('ctx', None, 'group'), may hold values from -0.5 to 0.5
- slab_adapter_index: int32 [8, 8], P('group'), may hold values from 0 to 255
- adapter_owner_slot: int32 [256], replicated, may hold values from 0 to 255, each once
Outputs:
- adapted: bfloat16 [65536, 4096], P(('group', 'ctx'))
Inputs may be any that keep to these rules, and one draw needn't show every extreme that they name: `slab_adapter_index`: a slab's list may name an adapter more than once. `adapter_owner_slot`: each slot once.
All inputs are finite; a program needn't handle non-finite values.
Results may differ from a plain program's by a relative error of at most 0.0054.
Values may be sent and summed in bfloat16 or wider, within the bound.
A program may use at most 64 MiB of HBM per device.

v0:
```python
import jax
import jax.numpy as jnp
from jax import lax
from jax.sharding import PartitionSpec as P


def spread(value, axis, source):
    kept = jnp.where(lax.axis_index(axis) == source, value, 0).astype(value.dtype)
    return lax.psum(kept, axis)


def causal_mix(signal, taps):
    width = taps.shape[0]
    kernel = taps[::-1][:, None, :]
    result = lax.conv_general_dilated(
        signal[None],
        kernel,
        (1,),
        [(width - 1, 0)],
        dimension_numbers=("NWC", "WIO", "NWC"),
        feature_group_count=signal.shape[1],
        precision=lax.Precision.HIGHEST,
    )
    return result[0]


def gather_slab_adapters(
    adapter_down_weight, adapter_up_weight, slab_adapter_index, adapter_owner_slot
):
    listed_all = lax.all_gather(slab_adapter_index, "group", axis=0, tiled=True)
    bank_size = adapter_owner_slot.shape[0]
    adapters_per_holder = adapter_down_weight.shape[0]
    count = listed_all.shape[1]
    matches = listed_all[:, :, None] == jnp.arange(bank_size, dtype=jnp.int32)[None, None, :]
    holder_slots = jnp.sum(jnp.where(matches, adapter_owner_slot[None, None, :], 0), axis=2)
    holder = holder_slots // adapters_per_holder
    local_slot = holder_slots % adapters_per_holder
    mine = holder == lax.axis_index("ctx")
    selected_adapters = (
        local_slot[:, :, None] == jnp.arange(adapters_per_holder, dtype=jnp.int32)[None, None, :]
    ) & mine[:, :, None]
    selected_adapters = selected_adapters.astype(jnp.bfloat16)
    down_pieces = jnp.einsum(
        "txc,cwf->txwf", selected_adapters, adapter_down_weight, preferred_element_type=jnp.float32
    ).astype(jnp.bfloat16)
    up_pieces = jnp.einsum(
        "txc,cwf->txwf", selected_adapters, adapter_up_weight, preferred_element_type=jnp.float32
    ).astype(jnp.bfloat16)
    down_recv, up_recv = (
        lax.all_to_all(down_pieces, "group", split_axis=0, concat_axis=0, tiled=True),
        lax.all_to_all(up_pieces, "group", split_axis=0, concat_axis=0, tiled=True),
    )
    low_rank_width = adapter_down_weight.shape[1]
    down_whole = jnp.transpose(down_recv, (1, 2, 0, 3)).reshape(count, low_rank_width, -1)
    up_whole = jnp.transpose(up_recv, (1, 2, 0, 3)).reshape(count, low_rank_width, -1)
    holder_mine = lax.dynamic_index_in_dim(holder, lax.axis_index("group"), 0, keepdims=False)
    down_list = []
    up_list = []
    for member in range(count):
        down_one, up_one = (
            spread(down_whole[member], "ctx", holder_mine[member]),
            spread(up_whole[member], "ctx", holder_mine[member]),
        )
        down_list.append(down_one)
        up_list.append(up_one)
    joined_down_maps = jnp.stack(down_list).reshape(count * low_rank_width, -1)
    joined_up_maps = jnp.stack(up_list).reshape(count * low_rank_width, -1)
    return (joined_down_maps, joined_up_maps)


def on_device(
    projected_queries,
    projected_keys,
    projected_values,
    short_filter_taps,
    long_filter_taps,
    adapter_down_weight,
    adapter_up_weight,
    slab_adapter_index,
    adapter_owner_slot,
):
    joined_down_maps, joined_up_maps = gather_slab_adapters(
        adapter_down_weight, adapter_up_weight, slab_adapter_index, adapter_owner_slot
    )
    query_cols, key_cols, value_cols = (
        lax.all_to_all(projected_queries, "ctx", split_axis=1, concat_axis=0, tiled=True),
        lax.all_to_all(projected_keys, "ctx", split_axis=1, concat_axis=0, tiled=True),
        lax.all_to_all(projected_values, "ctx", split_axis=1, concat_axis=0, tiled=True),
    )
    q_short = causal_mix(query_cols.astype(jnp.float32), short_filter_taps[0])
    k_short = causal_mix(key_cols.astype(jnp.float32), short_filter_taps[1])
    v_short = causal_mix(value_cols.astype(jnp.float32), short_filter_taps[2])
    gated = k_short * v_short
    long_conv = causal_mix(gated, long_filter_taps.astype(jnp.float32))
    mixed_cols = (q_short * long_conv).astype(jnp.bfloat16)
    mixed = lax.all_to_all(mixed_cols, "ctx", split_axis=0, concat_axis=1, tiled=True)
    low = jnp.einsum(
        "td,cd->tc", mixed, joined_down_maps, preferred_element_type=jnp.float32
    ).astype(jnp.bfloat16)
    total = mixed.astype(jnp.float32) + jnp.dot(
        low, joined_up_maps, preferred_element_type=jnp.float32
    )
    return total.astype(jnp.bfloat16)


def solution(mesh):
    in_specs = (
        P(("group", "ctx"), None),
        P(("group", "ctx"), None),
        P(("group", "ctx"), None),
        P(None, None, "ctx"),
        P(None, "ctx"),
        P("ctx", None, "group"),
        P("ctx", None, "group"),
        P("group", None),
        P(),
    )
    out_specs = P(("group", "ctx"), None)
    return jax.shard_map(
        on_device, mesh=mesh, in_specs=in_specs, out_specs=out_specs, check_vma=False
    )
```

profile of v0, /device:TPU:40, one launch (start us, length us, event | category | flops | bytes accessed | tf_op | source)
XLA Modules:
  0.0 640.7 jit_solution(14181144770218036884)
XLA Ops:
  6.5 10.8 %all-gather = s32[8,1,8]{2,1,0:T(1,128)S(1)} all-gather(s32[1,1,8]{2,1,0:T(1,128)} %bitcast.139), channel_id=1, replica_groups=mesh['group'=8,'ctx'=64] {'group'}, dimensions={0}, use_global_device_ids=true | all-gather | bytes 288 | tf_op jit(solution)/shard_map/all_gather | solution.py:30
  18.3 2.3 convolution_convert_fusion.1
  20.7 3.6 all-to-all-start.4
  25.7 14.4 %all-to-all-done.4 = bf16[8,8,16,512]{3,1,2,0:T(8,128)(2,1)S(1)} async-done(((bf16[8,8,16,512]{3,1,2,0:T(8,128)(2,1)}), bf16[8,8,16,512]{3,1,2,0:T(8,128)(2,1)S(1)}, u32[]{:S(2)}, u32[]{:S(2)}) %all-to-all-start.4) | async-done | bytes 1048608 | tf_op jit(solution)/shard_map/all_to_all | solution.py:50
  40.1 3.6 all-to-all-start.5
  45.0 14.5 %all-to-all-done.5 = bf16[8,8,16,512]{3,1,2,0:T(8,128)(2,1)S(1)} async-done(((bf16[8,8,16,512]{3,1,2,0:T(8,128)(2,1)}), bf16[8,8,16,512]{3,1,2,0:T(8,128)(2,1)S(1)}, u32[]{:S(2)}, u32[]{:S(2)}) %all-to-all-start.5) | async-done | bytes 1048608 | tf_op jit(solution)/shard_map/all_to_all | solution.py:51
  59.6 18.3 %all-to-all-start.1 = ((bf16[128,64,64]{0,2,1:T(8,128)(2,1)}), bf16[128,64,64]{0,2,1:T(8,128)(2,1)S(1)}, u32[]{:S(2)}, u32[]{:S(2)}) async-start(bf16[128,64,64]{0,2,1:T(8,128)(2,1)} %bitcast.128), calls=%async_computation.1 | async-start | bytes 2097152 | tf_op jit(solution)/shard_map/all_to_all | solution.py:87
  77.8 2.3 copy.100
  80.1 51.1 %all-to-all-done.1 = bf16[128,64,64]{0,2,1:T(8,128)(2,1)S(1)} async-done(((bf16[128,64,64]{0,2,1:T(8,128)(2,1)}), bf16[128,64,64]{0,2,1:T(8,128)(2,1)S(1)}, u32[]{:S(2)}, u32[]{:S(2)}) %all-to-all-start.1) | async-done | bytes 1048608 | tf_op jit(solution)/shard_map/all_to_all | solution.py:87
  131.2 7.2 %all-to-all-start.2 = ((bf16[128,64,64]{0,2,1:T(8,128)(2,1)}), bf16[128,64,64]{0,2,1:T(8,128)(2,1)}, u32[]{:S(2)}, u32[]{:S(2)}) async-start(bf16[128,64,64]{0,2,1:T(8,128)(2,1)} %bitcast.127), calls=%async_computation.2 | async-start | bytes 2097152 | tf_op jit(solution)/shard_map/all_to_all | solution.py:88
  144.1 3.7 broadcast_select_fusion.1
  156.7 3.4 broadcast_select_fusion
  170.3 21.5 %all-to-all-done.2 = bf16[128,64,64]{0,2,1:T(8,128)(2,1)} async-done(((bf16[128,64,64]{0,2,1:T(8,128)(2,1)}), bf16[128,64,64]{0,2,1:T(8,128)(2,1)}, u32[]{:S(2)}, u32[]{:S(2)}) %all-to-all-start.2) | async-done | bytes 1048608 | tf_op jit(solution)/shard_map/all_to_all | solution.py:88
  191.8 7.2 %all-to-all-start = ((bf16[128,64,64]{0,2,1:T(8,128)(2,1)}), bf16[128,64,64]{0,2,1:T(8,128)(2,1)}, u32[]{:S(2)}, u32[]{:S(2)}) async-start(bf16[128,64,64]{0,2,1:T(8,128)(2,1)} %bitcast), calls=%async_computation | async-start | bytes 2097152 | tf_op jit(solution)/shard_map/all_to_all | solution.py:86
  199.3 274.9 %all-reduce.3.cloned.1.call-done = (bf16[1,16,4096]{2,1,0:T(8,128)(2,1)}, bf16[1,16,4096]{2,1,0:T(8,128)(2,1)}, bf16[1,16,4096]{2,1,0:T(8,128)(2,1)}, bf16[1,16,...) async-done(((bf16[1,16,4096]{2,1,0:T(8,128)(2,1)}, ...) | async-done | bytes 2097168 | tf_op jit(solution)/shard_map/psum | solution.py:9
  475.1 1.6 constant_dynamic-update-slice_fusion.7
  481.9 1.5 reshape.181
  483.5 2.8 copy.98
  487.0 1.9 copy.101
  491.3 2.8 copy.103
  494.8 5.7 fusion.17
  500.5 1.9 select_bitcast_fusion
  502.4 2.0 copy-done.22
  505.2 1.9 copy.91
  509.5 2.8 copy.93
  513.1 5.9 fusion.13
  519.0 47.4 %multiply_convert_fusion = bf16[8,1025,64]{2,0,1:T(8,128)(2,1)} fusion(f32[8,1025,64]{2,0,1:T(8,128)S(1)} %fusion.13, pred[8,1025]{0,1:T(8,128)(4,1)S(1)} %copy-done.25, f32[128,1,64]{2,1,0:T(1,128)S(1)} %copy.105, f32[1,7,127,64]{3,1,2,0:T(8,128)S(1)} %copy-done.9, f32[1,8,1025,64]{3,1,2,0:T(8,128)S(1)} %bitcast.134), kind=kOutput, calls=%fused_computation.12 | convolution fusion | flops 809436672 | bytes 5516552 | tf_op jit(solution)/shard_map/conv_general_dilated | solution.py:15
  566.3 3.4 copy.106
  571.4 1.7 copy.107
  573.1 10.2 %all-to-all-start.3 = ((bf16[64,128,64]{1,2,0:T(8,128)(2,1)}), bf16[64,128,64]{1,2,0:T(8,128)(2,1)S(1)}, u32[]{:S(2)}, u32[]{:S(2)}) async-start(bf16[64,128,64]{1,2,0:T(8,128)(2,1)} %copy.107), calls=%async_computation.3 | async-start | bytes 2097152 | tf_op jit(solution)/shard_map/all_to_all | solution.py:96
  586.2 43.3 %all-to-all-done.3 = bf16[64,128,64]{1,2,0:T(8,128)(2,1)S(1)} async-done(((bf16[64,128,64]{1,2,0:T(8,128)(2,1)}), bf16[64,128,64]{1,2,0:T(8,128)(2,1)S(1)}, u32[]{:S(2)}, u32[]{:S(2)}) %all-to-all-start.3) | async-done | bytes 1048608 | tf_op jit(solution)/shard_map/all_to_all | solution.py:96
  630.1 3.5 fusion
  (136 shorter events, 42.3 us)
Async XLA Ops:
  6.5 17.7 %copy-start.21 = (bf16[4,16,512]{2,1,0:T(8,128)(2,1)S(1)}, bf16[4,16,512]{2,1,0:T(8,128)(2,1)}, u32[]{:S(2)}) copy-start(bf16[4,16,512]{2,1,0:T(8,128)(2,1)} %param.15) | copy-start | bytes 196612
  20.7 19.4 %all-to-all-start.4 = ((bf16[8,8,16,512]{3,1,2,0:T(8,128)(2,1)}), bf16[8,8,16,512]{3,1,2,0:T(8,128)(2,1)S(1)}, u32[]{:S(2)}, u32[]{:S(2)}) async-start(bf16[8,8,16,512]{3,1,2,0:T(8,128)(2,1)} %convolution_convert_fusion.1), calls=%async_computation.4 | async-start | bytes 2097152 | tf_op jit(solution)/shard_map/all_to_all | solution.py:50
  24.2 19.4 %copy-start.7 = (bf16[128,4096]{1,0:T(8,128)(2,1)S(1)}, bf16[128,4096]{1,0:T(8,128)(2,1)}, u32[]{:S(2)}) copy-start(bf16[128,4096]{1,0:T(8,128)(2,1)} %param.10) | copy-start | bytes 3145732
  40.1 19.5 %all-to-all-start.5 = ((bf16[8,8,16,512]{3,1,2,0:T(8,128)(2,1)}), bf16[8,8,16,512]{3,1,2,0:T(8,128)(2,1)S(1)}, u32[]{:S(2)}, u32[]{:S(2)}) async-start(bf16[8,8,16,512]{3,1,2,0:T(8,128)(2,1)} %convolution_convert_fusion), calls=%async_computation.5 | async-start | bytes 2097152 | tf_op jit(solution)/shard_map/all_to_all | solution.py:51
  59.6 71.7 %all-to-all-start.1 = ((bf16[128,64,64]{0,2,1:T(8,128)(2,1)}), bf16[128,64,64]{0,2,1:T(8,128)(2,1)S(1)}, u32[]{:S(2)}, u32[]{:S(2)}) async-start(bf16[128,64,64]{0,2,1:T(8,128)(2,1)} %bitcast.128), calls=%async_computation.1 | async-start | bytes 2097152 | tf_op jit(solution)/shard_map/all_to_all | solution.py:87
  131.2 60.6 %all-to-all-start.2 = ((bf16[128,64,64]{0,2,1:T(8,128)(2,1)}), bf16[128,64,64]{0,2,1:T(8,128)(2,1)}, u32[]{:S(2)}, u32[]{:S(2)}) async-start(bf16[128,64,64]{0,2,1:T(8,128)(2,1)} %bitcast.127), calls=%async_computation.2 | async-start | bytes 2097152 | tf_op jit(solution)/shard_map/all_to_all | solution.py:88
  138.5 335.7 %all-reduce.3.cloned.1.call-start = ((), (), s32[]{:S(2)}) async-start(), calls=%async_computation.6 | async-start | bytes 4194304 | tf_op jit(solution)/shard_map/psum | solution.py:9
  147.9 4.5 copy-start.6
  147.9 5.4 copy-start.5
  147.9 6.2 copy-start.4
  147.9 7.1 %copy-start.3 = (bf16[1,16,8,512]{3,0,1,2:T(2,128)(2,1)S(1)}, bf16[1,16,8,512]{3,0,1,2:T(2,128)(2,1)}, u32[]{:S(2)}) copy-start(bf16[1,16,8,512]{3,0,1,2:T(2,128)(2,1)} %get-tuple-element.24) | copy-start | bytes 393220
  169.0 30.1 %copy-start.24 = (f32[3,3,64]{2,1,0:T(4,128)S(1)}, f32[3,3,64]{2,1,0:T(4,128)}, u32[]{:S(2)}) copy-start(f32[3,3,64]{2,1,0:T(4,128)} %param.12) | copy-start | bytes 6916
  169.0 30.1 %copy-start.23 = (bf16[128,64]{0,1:T(8,128)(2,1)S(1)}, bf16[128,64]{0,1:T(8,128)(2,1)}, u32[]{:S(2)}) copy-start(bf16[128,64]{0,1:T(8,128)(2,1)} %param.13) | copy-start | bytes 49156
  191.8 313.4 %all-to-all-start = ((bf16[128,64,64]{0,2,1:T(8,128)(2,1)}), bf16[128,64,64]{0,2,1:T(8,128)(2,1)}, u32[]{:S(2)}, u32[]{:S(2)}) async-start(bf16[128,64,64]{0,2,1:T(8,128)(2,1)} %bitcast), calls=%async_computation | async-start | bytes 2097152 | tf_op jit(solution)/shard_map/all_to_all | solution.py:86
  494.8 5.7 copy-start
  494.8 5.7 copy-start.25
  509.5 9.4 %slice-start = ((s8[4198400]{0:T(1024)(128)(4,1)}), s8[4096]{0:T(1024)(128)(4,1)S(1)}, s32[]{:S(2)}) async-start(s8[4198400]{0:T(1024)(128)(4,1)} %bitcast.133), calls=%async_computation.7 | async-start | bytes 8192
  513.1 5.9 copy-start.9
  513.1 5.9 slice-start.1
  571.3 12.0 %copy-start.18 = (bf16[1,16,4096]{2,1,0:T(8,128)(2,1)S(1)}, bf16[1,16,4096]{2,1,0:T(8,128)(2,1)}, u32[]{:S(2)}) copy-start(bf16[1,16,4096]{2,1,0:T(8,128)(2,1)} %get-tuple-element.9) | copy-start | bytes 393220
  571.3 12.7 %copy-start.17 = (bf16[1,16,4096]{2,1,0:T(8,128)(2,1)S(1)}, bf16[1,16,4096]{2,1,0:T(8,128)(2,1)}, u32[]{:S(2)}) copy-start(bf16[1,16,4096]{2,1,0:T(8,128)(2,1)} %get-tuple-element.10) | copy-start | bytes 393220
  571.4 13.3 %copy-start.16 = (bf16[1,16,4096]{2,1,0:T(8,128)(2,1)S(1)}, bf16[1,16,4096]{2,1,0:T(8,128)(2,1)}, u32[]{:S(2)}) copy-start(bf16[1,16,4096]{2,1,0:T(8,128)(2,1)} %get-tuple-element.11) | copy-start | bytes 393220
  571.4 14.0 %copy-start.1 = (bf16[8,16,4096]{2,1,0:T(8,128)(2,1)S(1)}, bf16[8,16,4096]{2,1,0:T(8,128)(2,1)}, u32[]{:S(2)}) copy-start(bf16[8,16,4096]{2,1,0:T(8,128)(2,1)} %constant_dynamic-update-slice_fusion.7) | copy-start | bytes 3145732
  571.4 14.0 %copy-start.15 = (bf16[1,16,4096]{2,1,0:T(8,128)(2,1)S(1)}, bf16[1,16,4096]{2,1,0:T(8,128)(2,1)}, u32[]{:S(2)}) copy-start(bf16[1,16,4096]{2,1,0:T(8,128)(2,1)} %get-tuple-element.14) | copy-start | bytes 393220
  571.4 14.0 %copy-start.14 = (bf16[1,16,4096]{2,1,0:T(8,128)(2,1)S(1)}, bf16[1,16,4096]{2,1,0:T(8,128)(2,1)}, u32[]{:S(2)}) copy-start(bf16[1,16,4096]{2,1,0:T(8,128)(2,1)} %get-tuple-element.15) | copy-start | bytes 393220
  573.1 12.3 %copy-start.13 = (bf16[1,16,4096]{2,1,0:T(8,128)(2,1)S(1)}, bf16[1,16,4096]{2,1,0:T(8,128)(2,1)}, u32[]{:S(2)}) copy-start(bf16[1,16,4096]{2,1,0:T(8,128)(2,1)} %get-tuple-element.16) | copy-start | bytes 393220
  573.1 12.3 %copy-start.12 = (bf16[1,16,4096]{2,1,0:T(8,128)(2,1)S(1)}, bf16[1,16,4096]{2,1,0:T(8,128)(2,1)}, u32[]{:S(2)}) copy-start(bf16[1,16,4096]{2,1,0:T(8,128)(2,1)} %get-tuple-element.17) | copy-start | bytes 393220
  573.1 12.4 %copy-start.11 = (bf16[1,16,4096]{2,1,0:T(8,128)(2,1)S(1)}, bf16[1,16,4096]{2,1,0:T(8,128)(2,1)}, u32[]{:S(2)}) copy-start(bf16[1,16,4096]{2,1,0:T(8,128)(2,1)} %get-tuple-element.18) | copy-start | bytes 393220
  573.1 12.4 %copy-start.10 = (bf16[1,16,4096]{2,1,0:T(8,128)(2,1)S(1)}, bf16[1,16,4096]{2,1,0:T(8,128)(2,1)}, u32[]{:S(2)}) copy-start(bf16[1,16,4096]{2,1,0:T(8,128)(2,1)} %get-tuple-element.19) | copy-start | bytes 393220
  573.1 12.4 %copy-start.19 = (bf16[1,16,4096]{2,1,0:T(8,128)(2,1)S(1)}, bf16[1,16,4096]{2,1,0:T(8,128)(2,1)}, u32[]{:S(2)}) copy-start(bf16[1,16,4096]{2,1,0:T(8,128)(2,1)} %get-tuple-element.12) | copy-start | bytes 393220
  573.1 12.4 %copy-start.20 = (bf16[1,16,4096]{2,1,0:T(8,128)(2,1)S(1)}, bf16[1,16,4096]{2,1,0:T(8,128)(2,1)}, u32[]{:S(2)}) copy-start(bf16[1,16,4096]{2,1,0:T(8,128)(2,1)} %get-tuple-element.20) | copy-start | bytes 393220
  573.1 56.4 %all-to-all-start.3 = ((bf16[64,128,64]{1,2,0:T(8,128)(2,1)}), bf16[64,128,64]{1,2,0:T(8,128)(2,1)S(1)}, u32[]{:S(2)}, u32[]{:S(2)}) async-start(bf16[64,128,64]{1,2,0:T(8,128)(2,1)} %copy.107), calls=%async_computation.3 | async-start | bytes 2097152 | tf_op jit(solution)/shard_map/all_to_all | solution.py:96
  (3 other events, 5.6 us)
Sparse Core Ops, SparseCore 0:
  169.1 305.0 all-reduce.2
where the time goes:
time: 650 us; the launch traced here: 641 us
  waiting for transfers between devices  420 us (65%)
  matrix products  68.1 us (10%)
  local copies, waits for them, and re-layouts  64.5 us (10%)
  starting transfers between devices  50.1 us (8%)
  between operations  19.2 us (3%)
  blocking collectives  10.8 us (2%)
  other arithmetic  8.15 us (1%)
    psum x1, waiting for transfers between devices, spread(): return lax.psum(kept, axis)  275 us
    conv_general_dilated x4, matrix products, causal_mix(): lax.conv_general_dilated(signal[None], kernel, (1,), [(width - 1, 0)], di...  60.8 us
    all_to_all x1, waiting for transfers between devices, on_device(): lax.all_to_all(projected_keys, 'ctx', split_axis=1, concat_axis=0, tiled=...  51.1 us
    all_to_all x1, waiting for transfers between devices, on_device(): lax.all_to_all(mixed_cols, 'ctx', split_axis=0, concat_axis=1, tiled=True)  43.3 us
    all_to_all x1, waiting for transfers between devices, on_device(): lax.all_to_all(projected_values, 'ctx', split_axis=1, concat_axis=0, tile...  21.5 us
    all_to_all x1, starting transfers between devices, on_device(): lax.all_to_all(projected_keys, 'ctx', split_axis=1, concat_axis=0, tiled=...  18.3 us
    unnamed x75, local copies, waits for them, and re-layouts  15.6 us
    conv_general_dilated x9, local copies, waits for them, and re-layouts, causal_mix(): lax.conv_general_dilated(signal[None], kernel, (1,), [(width - 1, 0)], di...  15.1 us
  transfers between devices with their start and end apart: 7, of which 6 were waited for; matrix products, arithmetic and copies ran while one was open for 10% of the time, Pallas kernels for 0%

commit v1 on v0

v1 whole, which is shorter than its diff:
```python
import jax
import jax.numpy as jnp
import numpy as np
from jax import lax
from jax.experimental import pallas as pl
from jax.experimental.pallas import tpu as pltpu
from jax.sharding import PartitionSpec as P

MESH = pl.DeviceIdType.MESH
BF = jnp.bfloat16
F32 = jnp.float32
ROWS = 128
WIDTH = 4096
CHUNK = 512
CHUNKS = WIDTH // CHUNK
POINTS = 256
HALF = POINTS // 2


def split_high_low(matrix):
    high = matrix.astype(jnp.bfloat16)
    low = (matrix - high.astype(np.float64)).astype(jnp.bfloat16)
    return high, low


def transforms():
    row = np.arange(POINTS)
    angle = 2 * np.pi * np.outer(np.arange(HALF), row) / POINTS
    sine = -np.sin(angle)
    sine[0] = (-1.0) ** row
    forward = np.concatenate([np.cos(angle), sine], axis=0)
    back_cos = np.cos(angle[:, HALF:]).T * (2 / POINTS)
    back_cos[:, 0] = 1 / POINTS
    back_sine = -np.sin(angle[:, HALF:]).T * (2 / POINTS)
    back_sine[:, 0] = (-1.0) ** row[HALF:] / POINTS
    back = np.concatenate([back_cos, back_sine], axis=1)
    return split_high_low(forward) + split_high_low(back)


def place(y, z):
    return y * 16 + (z % 4) * 4 + z // 4


def dot(a, b):
    return lax.dot_general(a, b, (((1,), (0,)), ((), ())), preferred_element_type=F32)


def dot_nt(a, b):
    return lax.dot_general(a, b, (((1,), (1,)), ((), ())), preferred_element_type=F32)


def mixer_kernel(
    slots_ref, q_ref, k_ref, v_ref, tail_ref, short_ref, long_ref, down_ref, up_ref,
    fwd_hi, fwd_lo, back_hi, back_lo,
    out_ref,
    bank_d, bank_u, send_x, recv_x, part_b, sum_b, part_a, sum_a, fin,
    first_s, first_l, short_all, long_all, even_taps, odd_taps, tails, halo,
    gate_hi, gate_lo, spectrum, filt_re, filt_im, filt_re2, q_short, mixed,
    local_sem, tail_sem, halo_send, halo_recv, f_send, f_recv, a_send, a_recv,
):
    group = lax.axis_index("group")
    ctx = lax.axis_index("ctx")
    x, core = group // 2, group % 2
    y, z = ctx // 16, ctx % 16
    z_low, z_high = z % 4, z // 4
    has_before = ctx > 0

    def at_y(d):
        return (group, ((y + d) % 4) * 16 + z)

    def at_z(d):
        return (group, y * 16 + (z + d + 16) % 16)

    def at_x(d):
        return (((x + d) % 4) * 2 + core, ctx)

    def at_group(d):
        return ((group + d) % 8, ctx)

    after = (group, (ctx + 1) % 64)
    before = (group, (ctx + 63) % 64)

    barrier = pltpu.get_barrier_semaphore()
    peers = [at_y(d) for d in (1, 2, 3)] + [at_group(d) for d in range(1, 8)]
    peers += [at_z(d) for d in (1, -1, 2, -2, 4, -4, 8)] + [after, before]
    for peer in peers:
        pl.semaphore_signal(barrier, inc=1, device_id=peer, device_id_type=MESH)
    pl.semaphore_wait(barrier, len(peers))

    pending = []
    used = {"f": 0, "a": 0}

    def send(kind, src, dst, peer):
        at = used[kind]
        used[kind] += 1
        sems = (f_send, f_recv) if kind == "f" else (a_send, a_recv)
        copy = pltpu.make_async_remote_copy(
            src, dst, sems[0].at[at], sems[1].at[at], device_id=peer, device_id_type=MESH
        )
        copy.start()
        pending.append(copy)
        return copy

    def arrived(copies):
        for copy in copies:
            copy.wait_recv()

    tail_copy = pltpu.make_async_remote_copy(
        tail_ref, tails, tail_sem.at[0], tail_sem.at[1], device_id=after, device_id_type=MESH
    )
    tail_copy.start()
    round_f1 = []
    for d in (1, 2, 3):
        round_f1.append(send("f", short_ref, first_s.at[y], at_y(d)))
        round_f1.append(send("f", long_ref, first_l.at[y], at_y(d)))
    round_a1 = []
    for d in (1, 2, 3):
        round_a1.append(send("a", down_ref, bank_d.at[y], at_y(d)))
        round_a1.append(send("a", up_ref, bank_u.at[y], at_y(d)))
    first_s[y] = short_ref[...]
    first_l[y] = long_ref[...]
    bank_d[y] = down_ref[...]
    bank_u[y] = up_ref[...]

    arrived(round_f1)
    mine = place(x, z)
    round_f2 = []
    for d in (4, 8, -4):
        round_f2.append(send("f", first_s.at[x], short_all.at[mine], at_z(d)))
    for d in (4, 8, -4):
        round_f2.append(send("f", first_l.at[x], long_all.at[mine], at_z(d)))
    short_all[mine] = first_s[x]
    long_all[mine] = first_l[x]

    arrived(round_a1)
    round_a2 = []
    for d in range(8):
        slab = (group + d) % 8
        for e in range(2):
            slot = slots_ref[slab, y + 4 * e]
            keep = ((slot // 4) % 16 == z).astype(F32)
            down_one = (bank_d[slot // 64, slot % 4].astype(F32) * keep).astype(BF)
            up_one = (bank_u[slot // 64, slot % 4].astype(F32) * keep).astype(BF)
            if d == 0:
                recv_x[e, group] = down_one
                recv_x[2 + e, group] = up_one
            else:
                send_x[d - 1, e] = down_one
                send_x[d - 1, 2 + e] = up_one
        if d:
            round_a2.append(send("a", send_x.at[d - 1], recv_x.at[:, group], at_group(d)))

    arrived(round_f2)
    quad = pl.ds(x * 16 + z_low * 4, 4)
    round_f3 = []
    for d in (1, -1, -2):
        round_f3.append(send("f", short_all.at[quad], short_all.at[quad], at_z(d)))
    for d in (1, -1, -2):
        round_f3.append(send("f", long_all.at[quad], long_all.at[quad], at_z(d)))

    arrived(round_a2)
    round_a3 = []
    for j, d in enumerate((1, -1, -2)):
        round_a3.append(send("a", recv_x.at[(z + d + 16) % 4], part_b.at[j], at_z(d)))

    arrived(round_f3)
    row16 = pl.ds(x * 16, 16)
    round_f4s = []
    for d in (1, 2, 3):
        round_f4s.append(send("f", short_all.at[row16], short_all.at[row16], at_x(d)))
    round_f4l = []
    for d in (1, 2, 3):
        round_f4l.append(send("f", long_all.at[row16], long_all.at[row16], at_x(d)))

    arrived(round_a3)
    for c in range(8):
        sum_b[c] = (
            recv_x[z_low, c].astype(F32) + part_b[0, c].astype(F32)
            + part_b[1, c].astype(F32) + part_b[2, c].astype(F32)
        ).astype(BF)
    round_a4 = []
    for j in (1, 2, 3):
        cols = pl.ds(pl.multiple_of(((z_high + j) % 4) * 128, 128), 128)
        round_a4.append(send("a", sum_b.at[:, :, cols], part_a.at[j - 1], at_z(4 * j)))

    tail_copy.wait_recv()
    arrived(round_f4s)
    lane = lax.broadcasted_iota(jnp.int32, (8, 128), 1)

    def unpack(m, carry):
        h = 2 * m
        one = short_all[place(h // 16, h % 16)]
        two = short_all[place((h + 1) // 16, (h + 1) % 16)]
        at = pl.ds(pl.multiple_of(m * 128, 128), 128)
        even_taps[:, at] = jnp.where(lane < 64, one, pltpu.roll(two, 64, 1))
        odd_taps[:, at] = jnp.where(lane < 64, pltpu.roll(one, 64, 1), two)
        return carry

    lax.fori_loop(0, WIDTH // 128, unpack, 0)
    row = lax.broadcasted_iota(jnp.int32, (ROWS, CHUNK), 0)

    def short_filter(ref, stream, at):
        signal = ref[:, at].astype(F32)
        edge = jnp.where(has_before, tails[:, at].astype(F32), 0.0)
        older, newer = edge[2 * stream:2 * stream + 1], edge[2 * stream + 1:2 * stream + 2]
        back1 = jnp.where(row == 0, newer, pltpu.roll(signal, 1, 0))
        back2 = jnp.where(row == 0, older, jnp.where(row == 1, newer, pltpu.roll(signal, 2, 0)))
        total = None
        for j, shifted in enumerate((signal, back1, back2)):
            n = 3 * stream + j
            taps = (even_taps if n % 2 == 0 else odd_taps)[n // 2:n // 2 + 1, at]
            total = taps * shifted if total is None else total + taps * shifted
        return total

    def columns(c):
        return pl.ds(pl.multiple_of(c * CHUNK, CHUNK), CHUNK)

    def halo_copy(c):
        at = columns(c)
        return pltpu.make_async_remote_copy(
            gate_hi.at[:, at], halo.at[:, at], halo_send.at[c], halo_recv.at[c],
            device_id=after, device_id_type=MESH,
        )

    def gate(c, carry):
        at = columns(c)
        gated = short_filter(k_ref, 1, at) * short_filter(v_ref, 2, at)
        high = gated.astype(BF)
        gate_hi[:, at] = high
        gate_lo[:, at] = (gated - high.astype(F32)).astype(BF)
        halo_copy(c).start()
        return carry

    lax.fori_loop(0, CHUNKS, gate, 0)

    arrived(round_a4)
    own = pl.ds(pl.multiple_of(z_high * 128, 128), 128)
    for c in range(8):
        total = (
            sum_b[c, :, own].astype(F32) + part_a[0, c].astype(F32)
            + part_a[1, c].astype(F32) + part_a[2, c].astype(F32)
        ).astype(BF)
        sum_a[c] = total
        fin[z_low, y, c, :, own] = total
    round_a5 = []
    for j in (1, 2, 3):
        round_a5.append(send("a", sum_a, fin.at[z_low, y, :, :, own], at_z(4 * j)))

    arrived(round_f4l)

    def own_rows(c, carry):
        at = columns(c)
        q_short[:, at] = short_filter(q_ref, 0, at)
        high, low = gate_hi[:, at], gate_lo[:, at]
        spectrum[:, at] = (
            dot(fwd_hi[:, HALF:], high) + dot(fwd_lo[:, HALF:], high) + dot(fwd_hi[:, HALF:], low)
        )
        blocks = []
        for i in range(8):
            blocks.append(long_all[place(c // 2, 8 * (c % 2) + i)])
        taps = jnp.concatenate(blocks, axis=0)
        filt = dot_nt(fwd_hi[:, :HALF], taps) + dot_nt(fwd_lo[:, :HALF], taps)
        re, im = filt[:HALF], filt[HALF:]
        filt_re[:, at] = re
        filt_im[:, at] = jnp.where(row == 0, 0.0, im)
        filt_re2[:, at] = jnp.where(row == 0, im, re)
        return carry

    lax.fori_loop(0, 4, own_rows, 0)
    arrived(round_a5)
    round_a6 = []
    for d in (1, -1, -2):
        round_a6.append(send("a", fin.at[z_low, y], fin.at[z_low, y], at_z(d)))
    round_a7 = []
    for d in (1, 2, 3):
        round_a7.append(send("a", fin.at[z_low, y], fin.at[z_low, y], at_y(d)))
    lax.fori_loop(4, CHUNKS, own_rows, 0)
    for copy, d in zip(round_a6, (-1, 1, 2)):
        copy.wait_recv()
        k = (z + d + 16) % 4
        for e in (1, 2, 3):
            round_a7.append(send("a", fin.at[k, y], fin.at[k, y], at_y(e)))

    def mix(c, carry):
        at = columns(c)
        halo_copy(c).wait_recv()
        old = jnp.where(has_before, halo[:, at].astype(F32), 0.0).astype(BF)
        total = spectrum[:, at] + dot(fwd_hi[:, :HALF], old) + dot(fwd_lo[:, :HALF], old)
        re, im = total[:HALF], total[HALF:]
        f_im = filt_im[:, at]
        prod_re = re * filt_re[:, at] - im * f_im
        prod_im = re * f_im + im * filt_re2[:, at]
        re_hi, im_hi = prod_re.astype(BF), prod_im.astype(BF)
        re_lo = (prod_re - re_hi.astype(F32)).astype(BF)
        im_lo = (prod_im - im_hi.astype(F32)).astype(BF)
        high = jnp.concatenate([re_hi, im_hi], axis=0)
        low = jnp.concatenate([re_lo, im_lo], axis=0)
        long_conv = dot(back_hi[...], high) + dot(back_lo[...], high) + dot(back_hi[...], low)
        mixed[:, at] = (q_short[:, at] * long_conv).astype(BF)
        return carry

    lax.fori_loop(0, CHUNKS, mix, 0)

    arrived(round_a7)

    def down(c, total):
        maps = fin[pl.ds(0, 2), :, c].reshape(ROWS, CHUNK)
        return total + dot_nt(mixed[:, columns(c)], maps)

    low_rank = lax.fori_loop(0, CHUNKS, down, jnp.zeros((ROWS, ROWS), F32)).astype(BF)

    def up(c, carry):
        maps = fin[pl.ds(2, 2), :, c].reshape(ROWS, CHUNK)
        at = columns(c)
        out_ref[:, at] = (mixed[:, at].astype(F32) + dot(low_rank, maps)).astype(BF)
        return carry

    lax.fori_loop(0, CHUNKS, up, 0)

    tail_copy.wait_send()
    for copy in pending:
        copy.wait_send()

    def drain(c, carry):
        halo_copy(c).wait_send()
        return carry

    lax.fori_loop(0, CHUNKS, drain, 0)


def on_device(
    projected_queries,
    projected_keys,
    projected_values,
    short_filter_taps,
    long_filter_taps,
    adapter_down_weight,
    adapter_up_weight,
    slab_adapter_index,
    adapter_owner_slot,
):
    listed = lax.all_gather(slab_adapter_index, "group", axis=0, tiled=True)
    bank = jnp.arange(adapter_owner_slot.shape[0], dtype=jnp.int32)
    slots = jnp.sum(
        jnp.where(listed[:, :, None] == bank, adapter_owner_slot[None, None, :], 0), axis=2
    )
    tail = jnp.concatenate(
        [projected_queries[ROWS - 2:], projected_keys[ROWS - 2:], projected_values[ROWS - 2:]]
        + [jnp.zeros((10, WIDTH), BF)],
        axis=0,
    )
    short = jnp.pad(short_filter_taps.reshape(9, 64), ((0, 7), (0, 0))).reshape(8, 128)
    constants = [jnp.asarray(part) for part in transforms()]
    vmem = pl.BlockSpec(memory_space=pltpu.VMEM)
    return pl.pallas_call(
        mixer_kernel,
        out_shape=jax.ShapeDtypeStruct((ROWS, WIDTH), BF),
        in_specs=[pl.BlockSpec(memory_space=pltpu.SMEM)] + [vmem] * 12,
        out_specs=vmem,
        scratch_shapes=[
            pltpu.VMEM((4, 4, 16, CHUNK), BF),
            pltpu.VMEM((4, 4, 16, CHUNK), BF),
            pltpu.VMEM((7, 4, 16, CHUNK), BF),
            pltpu.VMEM((4, 8, 16, CHUNK), BF),
            pltpu.VMEM((3, 8, 16, CHUNK), BF),
            pltpu.VMEM((8, 16, CHUNK), BF),
            pltpu.VMEM((3, 8, 16, 128), BF),
            pltpu.VMEM((8, 16, 128), BF),
            pltpu.VMEM((4, 4, 8, 16, CHUNK), BF),
            pltpu.VMEM((4, 8, 128), F32),
            pltpu.VMEM((4, 64, 128), BF),
            pltpu.VMEM((64, 8, 128), F32),
            pltpu.VMEM((64, 64, 128), BF),
            pltpu.VMEM((8, WIDTH), F32),
            pltpu.VMEM((8, WIDTH), F32),
            pltpu.VMEM((16, WIDTH), BF),
            pltpu.VMEM((ROWS, WIDTH), BF),
            pltpu.VMEM((ROWS, WIDTH), BF),
            pltpu.VMEM((ROWS, WIDTH), BF),
            pltpu.VMEM((POINTS, WIDTH), F32),
            pltpu.VMEM((HALF, WIDTH), F32),
            pltpu.VMEM((HALF, WIDTH), F32),
            pltpu.VMEM((HALF, WIDTH), F32),
            pltpu.VMEM((ROWS, WIDTH), F32),
            pltpu.VMEM((ROWS, WIDTH), BF),
            pltpu.SemaphoreType.DMA((2,)),
            pltpu.SemaphoreType.DMA((2,)),
            pltpu.SemaphoreType.DMA((CHUNKS,)),
            pltpu.SemaphoreType.DMA((CHUNKS,)),
            pltpu.SemaphoreType.DMA((24,)),
            pltpu.SemaphoreType.DMA((24,)),
            pltpu.SemaphoreType.DMA((37,)),
            pltpu.SemaphoreType.DMA((37,)),
        ],
        compiler_params=pltpu.CompilerParams(
            collective_id=0, has_side_effects=True, vmem_limit_bytes=56 * 1024 * 1024
        ),
        cost_estimate=pl.CostEstimate(
            flops=3_000_000_000, bytes_accessed=8_000_000, transcendentals=0
        ),
    )(
        slots, projected_queries, projected_keys, projected_values, tail, short,
        long_filter_taps.T, adapter_down_weight, adapter_up_weight, *constants,
    )


def solution(mesh):
    in_specs = (
        P(("group", "ctx"), None),
        P(("group", "ctx"), None),
        P(("group", "ctx"), None),
        P(None, None, "ctx"),
        P(None, "ctx"),
        P("ctx", None, "group"),
        P("ctx", None, "group"),
        P("group", None),
        P(),
    )
    out_specs = P(("group", "ctx"), None)
    return jax.shard_map(
        on_device, mesh=mesh, in_specs=in_specs, out_specs=out_specs, check_vma=False
    )
```

time: 650 us -> 132 us (0.20)
  the two profiles are of different devices: /device:TPU:40 before, /device:TPU:84 now
where the time goes in v1:
time: 132 us
  Pallas kernels  116 us (88%)
  blocking collectives  8.45 us (6%)
  local copies, waits for them, and re-layouts  6.21 us (5%)
  other arithmetic  1.62 us (1%)
    pallas_call x1, Pallas kernels, on_device(): pl.pallas_call(mixer_kernel, out_shape=jax.ShapeDtypeStruct((ROWS, WIDTH)...  116 us
    all_gather x1, blocking collectives, on_device(): listed = lax.all_gather(slab_adapter_index, 'group', axis=0, tiled=True)  8.45 us
    unnamed x7, local copies, waits for them, and re-layouts  2.87 us

profile of v1, /device:TPU:84, one launch (start us, length us, event | category | flops | bytes accessed | tf_op | source)
XLA Modules:
  0.0 131.9 jit_solution(527700304961859454)
XLA Ops:
  0.0 0.0 copy-start.2
  0.0 0.1 pad.8.clone
  0.1 0.6 copy-done.2
  0.7 0.0 copy-start.1
  0.7 8.4 %all-gather = s32[8,1,8]{2,1,0:T(1,128)S(1)} all-gather(s32[1,1,8]{2,1,0:T(1,128)S(1)} %bitcast.4), channel_id=1, replica_groups=mesh['group'=8,'ctx'=64] {'group'}, dimensions={0}, use_global_device_ids=true | all-gather | bytes 288 | tf_op jit(solution)/shard_map/all_gather | solution.py:342
  9.1 0.0 copy-start
  9.1 0.0 copy-done.1
  9.1 0.9 select_reduce_fusion.slots_ref
  10.0 0.0 copy-done
  10.0 0.7 reshape.9.short_ref
  10.7 0.9 slice.9
  11.5 0.9 slice.10
  12.4 0.9 slice.11
  13.3 0.7 maximum_maximum_fusion.tail_ref
  14.0 115.6 %shard_map.127 = bf16[128,4096]{1,0:T(8,128)(2,1)} custom-call(s32[8,8]{1,0:T(8,128)} %select_reduce_fusion.slots_ref, bf16[128,4096]{1,0:T(8,128)(2,1)} %q_ref.1, bf16[128,4096]{1,0:T(8,128)(2,1)} %k_ref.1, bf16[128,4096]{1,0:T(8,128)(2,1)} %v_ref.1, bf16[16,4096]{1,0:T(8,128)(2,1)} %maximum_maximum_fusion.tail_ref, f32[8,128]{1,0:T(8,128)} %reshape.9.short_ref, ...), custom_call_target="tpu_custom_call" | custom-call | flops 3000000000 | bytes 8000000 | tf_op jit(solution)/shard_map/pallas_call | solution.py:355
  129.6 2.3 %copy.15 = bf16[128,4096]{1,0:T(8,128)(2,1)} copy(bf16[128,4096]{1,0:T(8,128)(2,1)} %shard_map.127) | data formatting | bytes 2097152
  (3 shorter events, 0.0 us)
Async XLA Ops:
  0.0 0.7 copy-start.2
  0.7 8.5 %copy-start.1 = (s32[256]{0:T(256)S(1)}, s32[256]{0:T(256)}, u32[]{:S(2)}) copy-start(s32[256]{0:T(256)} %param.21) | copy-start | bytes 3076
  9.1 0.9 copy-start

commit v2 on v1

v2 whole, which is shorter than its diff:
```python
import jax
import jax.numpy as jnp
import numpy as np
from jax import lax
from jax.experimental import pallas as pl
from jax.experimental.pallas import tpu as pltpu
from jax.sharding import PartitionSpec as P

MESH = pl.DeviceIdType.MESH
BF = jnp.bfloat16
F32 = jnp.float32
ROWS = 128
WIDTH = 4096
CHUNK = 512
CHUNKS = WIDTH // CHUNK
POINTS = 256
HALF = POINTS // 2


def split_high_low(matrix):
    high = matrix.astype(jnp.bfloat16)
    low = (matrix - high.astype(np.float64)).astype(jnp.bfloat16)
    return high, low


def transforms():
    row = np.arange(POINTS)
    angle = 2 * np.pi * np.outer(np.arange(HALF), row) / POINTS
    sine = -np.sin(angle)
    sine[0] = (-1.0) ** row
    forward = np.concatenate([np.cos(angle), sine], axis=0)
    back_cos = np.cos(angle[:, HALF:]).T * (2 / POINTS)
    back_cos[:, 0] = 1 / POINTS
    back_sine = -np.sin(angle[:, HALF:]).T * (2 / POINTS)
    back_sine[:, 0] = (-1.0) ** row[HALF:] / POINTS
    back = np.concatenate([back_cos, back_sine], axis=1)
    return split_high_low(forward) + split_high_low(back)


def dot(a, b):
    return lax.dot_general(a, b, (((1,), (0,)), ((), ())), preferred_element_type=F32)


def dot_nt(a, b):
    return lax.dot_general(a, b, (((1,), (1,)), ((), ())), preferred_element_type=F32)


def mixer_kernel(
    owner_ref, listed_ref, short_ref, long_ref, down_ref, up_ref,
    q_hbm, k_hbm, v_hbm, fwd_hi_hbm, fwd_lo_hbm, back_hi_hbm, back_lo_hbm,
    out_ref,
    q_ref, k_ref, v_ref, fwd_hi, fwd_lo, back_hi, back_lo,
    own_list, lists, slab_lists, bank_down, bank_up, send_x, recv_x, part_b, sum_b, part_a, sum_a, fin,
    own_short, short_all, first_long, long_all, even_taps, odd_taps, own_tail, tails, halo,
    gate_hi, filt_re, filt_im, filt_re2, q_short, mixed,
    load_sem, list_sem, tail_sem, halo_send, halo_recv, f_send, f_recv, a_send, a_recv,
):
    group = lax.axis_index("group")
    ctx = lax.axis_index("ctx")
    x, core = group // 2, group % 2
    y, z = ctx // 16, ctx % 16
    z_low, z_high = z % 4, z // 4
    has_before = ctx > 0

    def at_y(d):
        return (group, ((y + d) % 4) * 16 + z)

    def at_z(d):
        return (group, y * 16 + (z + d + 16) % 16)

    def at_x(d):
        return (((x + d) % 4) * 2 + core, ctx)

    def at_group(d):
        return ((group + d) % 8, ctx)

    after = (group, (ctx + 1) % 64)
    before = (group, (ctx + 63) % 64)

    barrier = pltpu.get_barrier_semaphore()
    peers = [at_y(d) for d in (1, 2, 3)] + [at_group(d) for d in range(1, 8)]
    peers += [at_z(d) for d in range(1, 16)] + [after, before]
    for peer in peers:
        pl.semaphore_signal(barrier, inc=1, device_id=peer, device_id_type=MESH)

    sources = (q_hbm, k_hbm, v_hbm, fwd_hi_hbm, fwd_lo_hbm, back_hi_hbm, back_lo_hbm)
    places = (q_ref, k_ref, v_ref, fwd_hi, fwd_lo, back_hi, back_lo)
    loads = [
        pltpu.make_async_copy(src, dst, load_sem.at[i])
        for i, (src, dst) in enumerate(zip(sources, places))
    ]
    for load in loads:
        load.start()

    own_list[...] = jnp.broadcast_to(
        jnp.concatenate([listed_ref[...], jnp.zeros((1, 120), jnp.int32)], axis=1), (8, 128)
    )
    taps = [short_ref[n // 3, n % 3:n % 3 + 1, :] for n in range(9)]
    taps += [jnp.zeros((1, 64), F32)] * 7
    for r in range(8):
        own_short[r:r + 1, :] = jnp.concatenate(taps[2 * r:2 * r + 2], axis=1)
    short_all[ctx] = own_short[...]
    tail_row = lax.broadcasted_iota(jnp.int32, (16, CHUNK), 0)

    def columns(c):
        return pl.ds(pl.multiple_of(c * CHUNK, CHUNK), CHUNK)

    def pack_tail(c, carry):
        at = columns(c)
        last = [ref[ROWS - 16:, at].astype(F32) for ref in (q_ref, k_ref, v_ref)]
        packed = jnp.where(tail_row < 6, pltpu.roll(last[2], 6, 0), 0.0)
        packed = jnp.where(tail_row < 4, pltpu.roll(last[1], 4, 0), packed)
        packed = jnp.where(tail_row < 2, pltpu.roll(last[0], 2, 0), packed)
        own_tail[:, at] = packed.astype(BF)
        return carry

    first_long[y] = long_ref[...]
    bank = (bank_down, bank_up)
    bank_down[y] = down_ref[...]
    bank_up[y] = up_ref[...]
    for load in loads[:3]:
        load.wait()
    lax.fori_loop(0, CHUNKS, pack_tail, 0)
    pl.semaphore_wait(barrier, len(peers))

    pending = []
    used = {"f": 0, "a": 0}

    def send(kind, src, dst, peer):
        at = used[kind]
        used[kind] += 1
        sems = (f_send, f_recv) if kind == "f" else (a_send, a_recv)
        copy = pltpu.make_async_remote_copy(
            src, dst, sems[0].at[at], sems[1].at[at], device_id=peer, device_id_type=MESH
        )
        copy.start()
        pending.append(copy)
        return copy

    def arrived(copies):
        for copy in copies:
            copy.wait_recv()

    bank_y = [
        [send("a", (down_ref, up_ref)[m], bank[m].at[y], at_y(d)) for d in (1, 2, 3)]
        for m in range(2)
    ]
    listed_all = [send("f", own_list, lists.at[group], at_group(d)) for d in range(1, 8)]
    lists[group] = own_list[...]
    arrived(listed_all)
    to_scalar = pltpu.make_async_copy(lists, slab_lists, list_sem.at[0])
    to_scalar.start()
    to_scalar.wait()

    bank_x = []
    for m in range(2):
        arrived(bank_y[m])
        copies = []
        for d in range(8):
            slab = (group + d) % 8
            for e in range(2):
                slot = owner_ref[slab_lists[slab, 0, y + 4 * e]]
                keep = ((slot // 4) % 16 == z).astype(F32)
                one = (bank[m][slot // 64, slot % 4].astype(F32) * keep).astype(BF)
                if d == 0:
                    recv_x[m, e, group // 4, group % 4] = one
                else:
                    send_x[m, d - 1, e] = one
            if d:
                copies.append(send(
                    "a", send_x.at[m, d - 1], recv_x.at[m, :, group // 4, group % 4], at_group(d)
                ))
        bank_x.append(copies)

    short_z = [send("f", own_short, short_all.at[ctx], at_z(d)) for d in range(1, 16)]
    long_y = [send("f", long_ref, first_long.at[y], at_y(d)) for d in (1, 2, 3)]

    def send_near(m):
        arrived(bank_x[m])
        copies = []
        for j, d in enumerate((1, -1, -2)):
            to = (z + d + 16) % 4
            copies.append(send("a", recv_x.at[m, to // 2, to % 2], part_b.at[m, j], at_z(d)))
        return copies


    bank_near = [send_near(0)]
    bank_near.append(send_near(1))
    tail_copy = pltpu.make_async_remote_copy(
        own_tail, tails, tail_sem.at[0], tail_sem.at[1], device_id=after, device_id_type=MESH
    )
    tail_copy.start()
    arrived(short_z)
    row16 = pl.ds(y * 16, 16)
    short_y = [send("f", short_all.at[row16], short_all.at[row16], at_y(d)) for d in (1, 2, 3)]

    arrived(long_y)
    mine = x * 16 + z_low * 4 + z_high
    long_far = [send("f", first_long.at[x], long_all.at[mine], at_z(d)) for d in (4, 8, -4)]
    long_all[mine] = first_long[x]

    bank_far = []
    for m in range(2):
        arrived(bank_near[m])
        for c in range(4):
            sum_b[m, c] = (
                recv_x[m, z_low // 2, z_low % 2, c].astype(F32) + part_b[m, 0, c].astype(F32)
                + part_b[m, 1, c].astype(F32) + part_b[m, 2, c].astype(F32)
            ).astype(BF)
        copies = []
        for j in (1, 2, 3):
            cols = pl.ds(pl.multiple_of(((z_high + j) % 4) * 128, 128), 128)
            copies.append(send("a", sum_b.at[m, :, :, cols], part_a.at[m, j - 1], at_z(4 * j)))
        bank_far.append(copies)

    tail_copy.wait_recv()
    arrived(short_y)
    lane = lax.broadcasted_iota(jnp.int32, (8, 128), 1)

    def unpack(i, carry):
        one, two = short_all[2 * i], short_all[2 * i + 1]
        at = pl.ds(pl.multiple_of(i * 128, 128), 128)
        even_taps[:, at] = jnp.where(lane < 64, one, pltpu.roll(two, 64, 1))
        odd_taps[:, at] = jnp.where(lane < 64, pltpu.roll(one, 64, 1), two)
        return carry

    lax.fori_loop(0, WIDTH // 128, unpack, 0)
    row = lax.broadcasted_iota(jnp.int32, (ROWS, CHUNK), 0)

    def short_filter(ref, stream, at):
        signal = ref[:, at].astype(F32)
        edge = jnp.where(has_before, tails[:, at].astype(F32), 0.0)
        older, newer = edge[2 * stream:2 * stream + 1], edge[2 * stream + 1:2 * stream + 2]
        back1 = jnp.where(row == 0, newer, pltpu.roll(signal, 1, 0))
        back2 = jnp.where(row == 0, older, jnp.where(row == 1, newer, pltpu.roll(signal, 2, 0)))
        total = None
        for j, shifted in enumerate((signal, back1, back2)):
            n = 3 * stream + j
            taps = (even_taps if n % 2 == 0 else odd_taps)[n // 2:n // 2 + 1, at]
            total = taps * shifted if total is None else total + taps * shifted
        return total

    def halo_copy(c):
        at = columns(c)
        return pltpu.make_async_remote_copy(
            gate_hi.at[:, at], halo.at[:, at], halo_send.at[c], halo_recv.at[c],
            device_id=after, device_id_type=MESH,
        )

    def gate(c, carry):
        at = columns(c)
        gated = short_filter(k_ref, 1, at) * short_filter(v_ref, 2, at)
        gate_hi[:, at] = gated.astype(BF)
        return carry

    def send_halo(c, carry):
        halo_copy(c).start()
        return carry


    lax.fori_loop(0, CHUNKS, gate, 0)
    arrived(long_far)
    quad = pl.ds(x * 16 + z_low * 4, 4)
    long_near = [send("f", long_all.at[quad], long_all.at[quad], at_z(d)) for d in (1, -1, -2)]

    own = pl.ds(pl.multiple_of(z_high * 128, 128), 128)
    to_far = []
    for m in range(2):
        arrived(bank_far[m])
        for c in range(4):
            total = (
                sum_b[m, c, :, own].astype(F32) + part_a[m, 0, c].astype(F32)
                + part_a[m, 1, c].astype(F32) + part_a[m, 2, c].astype(F32)
            ).astype(BF)
            sum_a[m, c] = total
            fin[m, y, z_low // 2, z_low % 2, c, :, own] = total
        target = fin.at[m, y, z_low // 2, z_low % 2, :, :, own]
        to_far.append([send("a", sum_a.at[m], target, at_z(4 * j)) for j in (1, 2, 3)])

    for load in loads[3:]:
        load.wait()
    def own_rows(c, carry):
        at = columns(c)
        q_short[:, at] = short_filter(q_ref, 0, at)
        return carry

    lax.fori_loop(0, CHUNKS, own_rows, 0)

    arrived(long_near)
    row16x = pl.ds(x * 16, 16)
    long_x = [send("f", long_all.at[row16x], long_all.at[row16x], at_x(d)) for d in (1, 2, 3)]

    def block_of(m, from_y, near_z):
        k = (near_z + 16) % 4
        return fin.at[m, (from_y + 4) % 4, k // 2, k % 2]

    def to_near(m):
        block = block_of(m, y, z)
        return [send("a", block, block, at_z(d)) for d in (1, -1, -2)]

    def to_y(m, near_z):
        block = block_of(m, y, near_z)
        return [send("a", block, block, at_y(d)) for d in (1, 3)]

    near_in, y_in = [], []
    for m in range(2):
        arrived(to_far[m])
        near_in.append(to_near(m))
    y_in.append([to_y(0, z), to_y(1, z)])
    lax.fori_loop(0, CHUNKS, send_halo, 0)
    def mix(c, carry):
        at = columns(c)
        halo_copy(c).wait_recv()
        old = jnp.where(has_before, halo[:, at].astype(F32), 0.0).astype(BF)
        total = dot(fwd_hi[...], jnp.concatenate([old, gate_hi[:, at]], axis=0))
        re, im = total[:HALF], total[HALF:]
        f_im = filt_im[:, at]
        prod_re = re * filt_re[:, at] - im * f_im
        prod_im = re * f_im + im * filt_re2[:, at]
        re_hi, im_hi = prod_re.astype(BF), prod_im.astype(BF)
        re_lo = (prod_re - re_hi.astype(F32)).astype(BF)
        im_lo = (prod_im - im_hi.astype(F32)).astype(BF)
        high = jnp.concatenate([re_hi, im_hi], axis=0)
        low = jnp.concatenate([re_lo, im_lo], axis=0)
        long_conv = dot(back_hi[...], high) + dot(back_lo[...], high) + dot(back_hi[...], low)
        mixed[:, at] = (q_short[:, at] * long_conv).astype(BF)
        return carry

    for j, d in enumerate((-1, 1, 2)):
        pair = []
        for m in range(2):
            arrived([near_in[m][j]])
            pair.append(to_y(m, z + d))
        y_in.append(pair)

    arrived(long_x)

    def filters(c, carry):
        at = columns(c)
        blocks = []
        for i in range(8):
            from_z = 8 * (c % 2) + i
            blocks.append(long_all[(c // 2) * 16 + (from_z % 4) * 4 + from_z // 4])
        taps = jnp.concatenate(blocks, axis=0)
        filt = dot_nt(fwd_hi[:, :HALF], taps) + dot_nt(fwd_lo[:, :HALF], taps)
        re, im = filt[:HALF], filt[HALF:]
        filt_re[:, at] = re
        filt_im[:, at] = jnp.where(row == 0, 0.0, im)
        filt_re2[:, at] = jnp.where(row == 0, im, re)
        return carry

    lax.fori_loop(0, CHUNKS, filters, 0)

    def forward(j, d):
        (down_right, _), (_, up_left) = y_in[j]
        arrived([down_right])
        block = block_of(0, y - 1, z + d)
        down_two.append(send("a", block, block, at_y(1)))
        arrived([up_left])
        block = block_of(1, y + 1, z + d)
        up_two.append(send("a", block, block, at_y(3)))

    down_two, up_two = [], []
    for j, d in enumerate((0, -1, 1, 2)):
        forward(j, d)
        lax.fori_loop(j, j + 1, mix, 0)
    lax.fori_loop(4, CHUNKS, mix, 0)
    down_in = [pair[0][1] for pair in y_in] + down_two
    up_in = [pair[1][0] for pair in y_in] + up_two

    def maps(m, c):
        return fin[m, :, :, c // 4, c % 4].reshape(ROWS, CHUNK)

    arrived(down_in)

    def down(c, total):
        return total + dot_nt(mixed[:, columns(c)], maps(0, c))

    low_rank = lax.fori_loop(0, CHUNKS, down, jnp.zeros((ROWS, ROWS), F32)).astype(BF)
    arrived(up_in)

    def up(c, carry):
        at = columns(c)
        out_ref[:, at] = (mixed[:, at].astype(F32) + dot(low_rank, maps(1, c))).astype(BF)
        return carry

    lax.fori_loop(0, CHUNKS, up, 0)

    tail_copy.wait_send()
    for copy in pending:
        copy.wait_send()

    def drain(c, carry):
        halo_copy(c).wait_send()
        return carry

    lax.fori_loop(0, CHUNKS, drain, 0)


def on_device(
    projected_queries,
    projected_keys,
    projected_values,
    short_filter_taps,
    long_filter_taps,
    adapter_down_weight,
    adapter_up_weight,
    slab_adapter_index,
    adapter_owner_slot,
):
    constants = [jnp.asarray(part) for part in transforms()]
    vmem = pl.BlockSpec(memory_space=pltpu.VMEM)
    return pl.pallas_call(
        mixer_kernel,
        out_shape=jax.ShapeDtypeStruct((ROWS, WIDTH), BF),
        in_specs=(
            [pl.BlockSpec(memory_space=pltpu.SMEM)] + [vmem] * 5
            + [pl.BlockSpec(memory_space=pl.ANY)] * 7
        ),
        out_specs=vmem,
        scratch_shapes=[
            pltpu.VMEM((ROWS, WIDTH), BF),
            pltpu.VMEM((ROWS, WIDTH), BF),
            pltpu.VMEM((ROWS, WIDTH), BF),
            pltpu.VMEM((POINTS, POINTS), BF),
            pltpu.VMEM((POINTS, POINTS), BF),
            pltpu.VMEM((HALF, POINTS), BF),
            pltpu.VMEM((HALF, POINTS), BF),
            pltpu.VMEM((8, 128), jnp.int32),
            pltpu.VMEM((8, 8, 128), jnp.int32),
            pltpu.SMEM((8, 8, 128), jnp.int32),
            pltpu.VMEM((4, 4, 16, CHUNK), BF),
            pltpu.VMEM((4, 4, 16, CHUNK), BF),
            pltpu.VMEM((2, 7, 2, 16, CHUNK), BF),
            pltpu.VMEM((2, 2, 2, 4, 16, CHUNK), BF),
            pltpu.VMEM((2, 3, 4, 16, CHUNK), BF),
            pltpu.VMEM((2, 4, 16, CHUNK), BF),
            pltpu.VMEM((2, 3, 4, 16, 128), BF),
            pltpu.VMEM((2, 4, 16, 128), BF),
            pltpu.VMEM((2, 4, 2, 2, 4, 16, CHUNK), BF),
            pltpu.VMEM((8, 128), F32),
            pltpu.VMEM((64, 8, 128), F32),
            pltpu.VMEM((4, 64, 128), BF),
            pltpu.VMEM((64, 64, 128), BF),
            pltpu.VMEM((8, WIDTH), F32),
            pltpu.VMEM((8, WIDTH), F32),
            pltpu.VMEM((16, WIDTH), BF),
            pltpu.VMEM((16, WIDTH), BF),
            pltpu.VMEM((ROWS, WIDTH), BF),
            pltpu.VMEM((ROWS, WIDTH), BF),
            pltpu.VMEM((HALF, WIDTH), F32),
            pltpu.VMEM((HALF, WIDTH), F32),
            pltpu.VMEM((HALF, WIDTH), F32),
            pltpu.VMEM((ROWS, WIDTH), F32),
            pltpu.VMEM((ROWS, WIDTH), BF),
            pltpu.SemaphoreType.DMA((7,)),
            pltpu.SemaphoreType.DMA((1,)),
            pltpu.SemaphoreType.DMA((2,)),
            pltpu.SemaphoreType.DMA((CHUNKS,)),
            pltpu.SemaphoreType.DMA((CHUNKS,)),
            pltpu.SemaphoreType.DMA((37,)),
            pltpu.SemaphoreType.DMA((37,)),
            pltpu.SemaphoreType.DMA((68,)),
            pltpu.SemaphoreType.DMA((68,)),
        ],
        compiler_params=pltpu.CompilerParams(
            collective_id=0, has_side_effects=True, vmem_limit_bytes=56 * 1024 * 1024
        ),
        cost_estimate=pl.CostEstimate(
            flops=3_000_000_000, bytes_accessed=8_000_000, transcendentals=0
        ),
    )(
        adapter_owner_slot, slab_adapter_index, short_filter_taps, long_filter_taps.T,
        adapter_down_weight, adapter_up_weight, projected_queries, projected_keys,
        projected_values, *constants,
    )


def solution(mesh):
    in_specs = (
        P(("group", "ctx"), None),
        P(("group", "ctx"), None),
        P(("group", "ctx"), None),
        P(None, None, "ctx"),
        P(None, "ctx"),
        P("ctx", None, "group"),
        P("ctx", None, "group"),
        P("group", None),
        P(),
    )
    out_specs = P(("group", "ctx"), None)
    return jax.shard_map(
        on_device, mesh=mesh, in_specs=in_specs, out_specs=out_specs, check_vma=False
    )
```

time: 132 us -> 111 us (0.84)
  the two profiles are of different devices: /device:TPU:84 before, /device:TPU:1 now
where the time goes in v2:
time: 111 us
  Pallas kernels  109 us (98%)
  local copies, waits for them, and re-layouts  2.29 us (2%)
    pallas_call x1, Pallas kernels, on_device(): pl.pallas_call(mixer_kernel, out_shape=jax.ShapeDtypeStruct((ROWS, WIDTH)...  109 us
    unnamed x1, local copies, waits for them, and re-layouts  2.29 us

profile of v2, /device:TPU:1, one launch (start us, length us, event | category | flops | bytes accessed | tf_op | source)
XLA Modules:
  0.0 110.9 jit_solution(5684325679079436758)
XLA Ops:
  0.0 108.6 %shard_map.127 = bf16[128,4096]{1,0:T(8,128)(2,1)} custom-call(s32[256]{0:T(256)} %owner_ref.1, s32[1,8]{1,0:T(1,128)} %listed_ref.1, f32[3,3,64]{2,1,0:T(4,128)} %short_ref.1, bf16[64,128]{1,0:T(8,128)(2,1)} %bitcast.1, bf16[4,16,512]{2,1,0:T(8,128)(2,1)} %down_ref.1, bf16[4,16,512]{2,1,0:T(8,128)(2,1)} %up_ref.1, bf16[128,4096]{1,0:T(8,128)(2,1)} %q_hbm.1, ...), custom_call_target="tpu_custom_call" | custom-call | flops 3000000000 | bytes 8000000 | tf_op jit(solution)/shard_map/pallas_call | solution.py:413
  108.7 2.3 %copy.15 = bf16[128,4096]{1,0:T(8,128)(2,1)} copy(bf16[128,4096]{1,0:T(8,128)(2,1)} %shard_map.127) | data formatting | bytes 2097152

commit v3 on v2

--- a/solution.py
+++ b/solution.py
@@ -52,7 +52,7 @@
     q_ref, k_ref, v_ref, fwd_hi, fwd_lo, back_hi, back_lo,
     own_list, lists, slab_lists, bank_down, bank_up, send_x, recv_x, part_b, sum_b, part_a, sum_a, fin,
     own_short, short_all, first_long, long_all, even_taps, odd_taps, own_tail, tails, halo,
-    gate_hi, filt_re, filt_im, filt_re2, q_short, mixed,
+    gate_hi, gate_lo, spectrum, filt_re, filt_im, filt_re2, q_short, mixed,
     load_sem, list_sem, tail_sem, halo_send, halo_recv, f_send, f_recv, a_send, a_recv,
 ):
     group = lax.axis_index("group")
@@ -118,9 +118,6 @@
     bank = (bank_down, bank_up)
     bank_down[y] = down_ref[...]
     bank_up[y] = up_ref[...]
-    for load in loads[:3]:
-        load.wait()
-    lax.fori_loop(0, CHUNKS, pack_tail, 0)
     pl.semaphore_wait(barrier, len(peers))
 
     pending = []
@@ -145,8 +142,11 @@
         [send("a", (down_ref, up_ref)[m], bank[m].at[y], at_y(d)) for d in (1, 2, 3)]
         for m in range(2)
     ]
+    short_z = [send("f", own_short, short_all.at[ctx], at_z(d)) for d in range(1, 16)]
     listed_all = [send("f", own_list, lists.at[group], at_group(d)) for d in range(1, 8)]
     lists[group] = own_list[...]
+    long_y = [send("f", long_ref, first_long.at[y], at_y(d)) for d in (1, 2, 3)]
+
     arrived(listed_all)
     to_scalar = pltpu.make_async_copy(lists, slab_lists, list_sem.at[0])
     to_scalar.start()
@@ -172,8 +172,17 @@
                 ))
         bank_x.append(copies)
 
-    short_z = [send("f", own_short, short_all.at[ctx], at_z(d)) for d in range(1, 16)]
-    long_y = [send("f", long_ref, first_long.at[y], at_y(d)) for d in (1, 2, 3)]
+    for load in loads[:3]:
+        load.wait()
+    lax.fori_loop(0, CHUNKS, pack_tail, 0)
+    tail_copy = pltpu.make_async_remote_copy(
+        own_tail, tails, tail_sem.at[0], tail_sem.at[1], device_id=after, device_id_type=MESH
+    )
+    tail_copy.start()
+    arrived(long_y)
+    mine = x * 16 + z_low * 4 + z_high
+    long_far = [send("f", first_long.at[x], long_all.at[mine], at_z(d)) for d in (4, 8, -4)]
+    long_all[mine] = first_long[x]
 
     def send_near(m):
         arrived(bank_x[m])
@@ -185,20 +194,60 @@
 
 
     bank_near = [send_near(0)]
-    bank_near.append(send_near(1))
-    tail_copy = pltpu.make_async_remote_copy(
-        own_tail, tails, tail_sem.at[0], tail_sem.at[1], device_id=after, device_id_type=MESH
-    )
-    tail_copy.start()
     arrived(short_z)
     row16 = pl.ds(y * 16, 16)
     short_y = [send("f", short_all.at[row16], short_all.at[row16], at_y(d)) for d in (1, 2, 3)]
 
-    arrived(long_y)
-    mine = x * 16 + z_low * 4 + z_high
-    long_far = [send("f", first_long.at[x], long_all.at[mine], at_z(d)) for d in (4, 8, -4)]
-    long_all[mine] = first_long[x]
-
+    bank_near.append(send_near(1))
+    tail_copy.wait_recv()
+    arrived(short_y)
+    lane = lax.broadcasted_iota(jnp.int32, (8, 128), 1)
+
+    def unpack(i, carry):
+        one, two = short_all[2 * i], short_all[2 * i + 1]
+        at = pl.ds(pl.multiple_of(i * 128, 128), 128)
+        even_taps[:, at] = jnp.where(lane < 64, one, pltpu.roll(two, 64, 1))
+        odd_taps[:, at] = jnp.where(lane < 64, pltpu.roll(one, 64, 1), two)
+        return carry
+
+    lax.fori_loop(0, WIDTH // 128, unpack, 0)
+    row = lax.broadcasted_iota(jnp.int32, (ROWS, CHUNK), 0)
+
+    def short_filter(ref, stream, at):
+        signal = ref[:, at].astype(F32)
+        edge = jnp.where(has_before, tails[:, at].astype(F32), 0.0)
+        older, newer = edge[2 * stream:2 * stream + 1], edge[2 * stream + 1:2 * stream + 2]
+        back1 = jnp.where(row == 0, newer, pltpu.roll(signal, 1, 0))
+        back2 = jnp.where(row == 0, older, jnp.where(row == 1, newer, pltpu.roll(signal, 2, 0)))
+        total = None
+        for j, shifted in enumerate((signal, back1, back2)):
+            n = 3 * stream + j
+            taps = (even_taps if n % 2 == 0 else odd_taps)[n // 2:n // 2 + 1, at]
+            total = taps * shifted if total is None else total + taps * shifted
+        return total
+
+    def halo_copy(c):
+        at = columns(c)
+        return pltpu.make_async_remote_copy(
+            gate_hi.at[:, at], halo.at[:, at], halo_send.at[c], halo_recv.at[c],
+            device_id=after, device_id_type=MESH,
+        )
+
+    def gate(c, carry):
+        at = columns(c)
+        gated = short_filter(k_ref, 1, at) * short_filter(v_ref, 2, at)
+        high = gated.astype(BF)
+        gate_hi[:, at] = high
+        gate_lo[:, at] = (gated - high.astype(F32)).astype(BF)
+        return carry
+
+    def send_halo(c, carry):
+        halo_copy(c).start()
+        return carry
+
+
+    lax.fori_loop(0, 2, gate, 0)
+    lax.fori_loop(0, 2, send_halo, 0)
     bank_far = []
     for m in range(2):
         arrived(bank_near[m])
@@ -213,55 +262,24 @@
             copies.append(send("a", sum_b.at[m, :, :, cols], part_a.at[m, j - 1], at_z(4 * j)))
         bank_far.append(copies)
 
-    tail_copy.wait_recv()
-    arrived(short_y)
-    lane = lax.broadcasted_iota(jnp.int32, (8, 128), 1)
-
-    def unpack(i, carry):
-        one, two = short_all[2 * i], short_all[2 * i + 1]
-        at = pl.ds(pl.multiple_of(i * 128, 128), 128)
-        even_taps[:, at] = jnp.where(lane < 64, one, pltpu.roll(two, 64, 1))
-        odd_taps[:, at] = jnp.where(lane < 64, pltpu.roll(one, 64, 1), two)
-        return carry
-
-    lax.fori_loop(0, WIDTH // 128, unpack, 0)
-    row = lax.broadcasted_iota(jnp.int32, (ROWS, CHUNK), 0)
-
-    def short_filter(ref, stream, at):
-        signal = ref[:, at].astype(F32)
-        edge = jnp.where(has_before, tails[:, at].astype(F32), 0.0)
-        older, newer = edge[2 * stream:2 * stream + 1], edge[2 * stream + 1:2 * stream + 2]
-        back1 = jnp.where(row == 0, newer, pltpu.roll(signal, 1, 0))
-        back2 = jnp.where(row == 0, older, jnp.where(row == 1, newer, pltpu.roll(signal, 2, 0)))
-        total = None
-        for j, shifted in enumerate((signal, back1, back2)):
-            n = 3 * stream + j
-            taps = (even_taps if n % 2 == 0 else odd_taps)[n // 2:n // 2 + 1, at]
-            total = taps * shifted if total is None else total + taps * shifted
-        return total
-
-    def halo_copy(c):
-        at = columns(c)
-        return pltpu.make_async_remote_copy(
-            gate_hi.at[:, at], halo.at[:, at], halo_send.at[c], halo_recv.at[c],
-            device_id=after, device_id_type=MESH,
-        )
-
-    def gate(c, carry):
-        at = columns(c)
-        gated = short_filter(k_ref, 1, at) * short_filter(v_ref, 2, at)
-        gate_hi[:, at] = gated.astype(BF)
-        return carry
-
-    def send_halo(c, carry):
-        halo_copy(c).start()
-        return carry
-
-
-    lax.fori_loop(0, CHUNKS, gate, 0)
+    lax.fori_loop(2, CHUNKS, gate, 0)
+    lax.fori_loop(2, 5, send_halo, 0)
     arrived(long_far)
     quad = pl.ds(x * 16 + z_low * 4, 4)
     long_near = [send("f", long_all.at[quad], long_all.at[quad], at_z(d)) for d in (1, -1, -2)]
+
+    for load in loads[3:]:
+        load.wait()
+    def own_rows(c, carry):
+        at = columns(c)
+        q_short[:, at] = short_filter(q_ref, 0, at)
+        high, low = gate_hi[:, at], gate_lo[:, at]
+        spectrum[:, at] = (
+            dot(fwd_hi[:, HALF:], high) + dot(fwd_lo[:, HALF:], high) + dot(fwd_hi[:, HALF:], low)
+        )
+        return carry
+
+    lax.fori_loop(0, CHUNKS, own_rows, 0)
 
     own = pl.ds(pl.multiple_of(z_high * 128, 128), 128)
     to_far = []
@@ -277,42 +295,50 @@
         target = fin.at[m, y, z_low // 2, z_low % 2, :, :, own]
         to_far.append([send("a", sum_a.at[m], target, at_z(4 * j)) for j in (1, 2, 3)])
 
-    for load in loads[3:]:
-        load.wait()
-    def own_rows(c, carry):
-        at = columns(c)
-        q_short[:, at] = short_filter(q_ref, 0, at)
-        return carry
-
-    lax.fori_loop(0, CHUNKS, own_rows, 0)
-
+    lax.fori_loop(5, CHUNKS, send_halo, 0)
     arrived(long_near)
     row16x = pl.ds(x * 16, 16)
     long_x = [send("f", long_all.at[row16x], long_all.at[row16x], at_x(d)) for d in (1, 2, 3)]
 
-    def block_of(m, from_y, near_z):
-        k = (near_z + 16) % 4
-        return fin.at[m, (from_y + 4) % 4, k // 2, k % 2]
-
-    def to_near(m):
-        block = block_of(m, y, z)
-        return [send("a", block, block, at_z(d)) for d in (1, -1, -2)]
-
-    def to_y(m, near_z):
-        block = block_of(m, y, near_z)
-        return [send("a", block, block, at_y(d)) for d in (1, 3)]
-
-    near_in, y_in = [], []
+    to_near, to_y = [], [[], []]
     for m in range(2):
         arrived(to_far[m])
-        near_in.append(to_near(m))
-    y_in.append([to_y(0, z), to_y(1, z)])
-    lax.fori_loop(0, CHUNKS, send_halo, 0)
+        block = fin.at[m, y, z_low // 2, z_low % 2]
+        to_near.append([send("a", block, block, at_z(d)) for d in (1, -1, -2)])
+        to_y[m] += [send("a", block, block, at_y(d)) for d in (1, 2, 3)]
+
+    arrived(long_x)
+
+    def filters(c, carry):
+        at = columns(c)
+        blocks = []
+        for i in range(8):
+            from_z = 8 * (c % 2) + i
+            blocks.append(long_all[(c // 2) * 16 + (from_z % 4) * 4 + from_z // 4])
+        taps = jnp.concatenate(blocks, axis=0)
+        filt = dot_nt(fwd_hi[:, :HALF], taps) + dot_nt(fwd_lo[:, :HALF], taps)
+        re, im = filt[:HALF], filt[HALF:]
+        filt_re[:, at] = re
+        filt_im[:, at] = jnp.where(row == 0, 0.0, im)
+        filt_re2[:, at] = jnp.where(row == 0, im, re)
+        return carry
+
+    lax.fori_loop(0, CHUNKS, filters, 0)
+
+    def pass_on(m):
+        for copy, d in zip(to_near[m], (-1, 1, 2)):
+            arrived([copy])
+            k = (z + d + 16) % 4
+            block = fin.at[m, y, k // 2, k % 2]
+            to_y[m].extend([send("a", block, block, at_y(e)) for e in (1, 2, 3)])
+
+    pass_on(0)
+    pass_on(1)
     def mix(c, carry):
         at = columns(c)
         halo_copy(c).wait_recv()
         old = jnp.where(has_before, halo[:, at].astype(F32), 0.0).astype(BF)
-        total = dot(fwd_hi[...], jnp.concatenate([old, gate_hi[:, at]], axis=0))
+        total = spectrum[:, at] + dot(fwd_hi[:, :HALF], old) + dot(fwd_lo[:, :HALF], old)
         re, im = total[:HALF], total[HALF:]
         f_im = filt_im[:, at]
         prod_re = re * filt_re[:, at] - im * f_im
@@ -326,58 +352,18 @@
         mixed[:, at] = (q_short[:, at] * long_conv).astype(BF)
         return carry
 
-    for j, d in enumerate((-1, 1, 2)):
-        pair = []
-        for m in range(2):
-            arrived([near_in[m][j]])
-            pair.append(to_y(m, z + d))
-        y_in.append(pair)
-
-    arrived(long_x)
-
-    def filters(c, carry):
-        at = columns(c)
-        blocks = []
-        for i in range(8):
-            from_z = 8 * (c % 2) + i
-            blocks.append(long_all[(c // 2) * 16 + (from_z % 4) * 4 + from_z // 4])
-        taps = jnp.concatenate(blocks, axis=0)
-        filt = dot_nt(fwd_hi[:, :HALF], taps) + dot_nt(fwd_lo[:, :HALF], taps)
-        re, im = filt[:HALF], filt[HALF:]
-        filt_re[:, at] = re
-        filt_im[:, at] = jnp.where(row == 0, 0.0, im)
-        filt_re2[:, at] = jnp.where(row == 0, im, re)
-        return carry
-
-    lax.fori_loop(0, CHUNKS, filters, 0)
-
-    def forward(j, d):
-        (down_right, _), (_, up_left) = y_in[j]
-        arrived([down_right])
-        block = block_of(0, y - 1, z + d)
-        down_two.append(send("a", block, block, at_y(1)))
-        arrived([up_left])
-        block = block_of(1, y + 1, z + d)
-        up_two.append(send("a", block, block, at_y(3)))
-
-    down_two, up_two = [], []
-    for j, d in enumerate((0, -1, 1, 2)):
-        forward(j, d)
-        lax.fori_loop(j, j + 1, mix, 0)
-    lax.fori_loop(4, CHUNKS, mix, 0)
-    down_in = [pair[0][1] for pair in y_in] + down_two
-    up_in = [pair[1][0] for pair in y_in] + up_two
+    lax.fori_loop(0, CHUNKS, mix, 0)
 
     def maps(m, c):
         return fin[m, :, :, c // 4, c % 4].reshape(ROWS, CHUNK)
 
-    arrived(down_in)
+    arrived(to_y[0])
 
     def down(c, total):
         return total + dot_nt(mixed[:, columns(c)], maps(0, c))
 
     low_rank = lax.fori_loop(0, CHUNKS, down, jnp.zeros((ROWS, ROWS), F32)).astype(BF)
-    arrived(up_in)
+    arrived(to_y[1])
 
     def up(c, carry):
         at = columns(c)
@@ -448,6 +434,8 @@
             pltpu.VMEM((16, WIDTH), BF),
             pltpu.VMEM((ROWS, WIDTH), BF),
             pltpu.VMEM((ROWS, WIDTH), BF),
+            pltpu.VMEM((ROWS, WIDTH), BF),
+            pltpu.VMEM((POINTS, WIDTH), F32),
             pltpu.VMEM((HALF, WIDTH), F32),
             pltpu.VMEM((HALF, WIDTH), F32),
             pltpu.VMEM((HALF, WIDTH), F32),

time: 111 us -> 104 us (0.937)
  Pallas kernels: 109 us -> 102 us
    pallas_call x1, Pallas kernels: 109 us -> 102 us  [on_device(): pl.pallas_call(mixer_kernel, out_shape=jax.ShapeDtypeStruct((ROWS, WIDTH)...]
where the time goes in v3:
time: 104 us
  Pallas kernels  102 us (98%)
  local copies, waits for them, and re-layouts  2.29 us (2%)
    pallas_call x1, Pallas kernels, on_device(): pl.pallas_call(mixer_kernel, out_shape=jax.ShapeDtypeStruct((ROWS, WIDTH)...  102 us
    unnamed x1, local copies, waits for them, and re-layouts  2.29 us

profile of v3, /device:TPU:1, one launch (start us, length us, event | category | flops | bytes accessed | tf_op | source)
XLA Modules:
  0.0 104.2 jit_solution(9797180521325098260)
XLA Ops:
  0.0 101.9 %shard_map.127 = bf16[128,4096]{1,0:T(8,128)(2,1)} custom-call(s32[256]{0:T(256)} %owner_ref.1, s32[1,8]{1,0:T(1,128)} %listed_ref.1, f32[3,3,64]{2,1,0:T(4,128)} %short_ref.1, bf16[64,128]{1,0:T(8,128)(2,1)} %bitcast.1, bf16[4,16,512]{2,1,0:T(8,128)(2,1)} %down_ref.1, bf16[4,16,512]{2,1,0:T(8,128)(2,1)} %up_ref.1, bf16[128,4096]{1,0:T(8,128)(2,1)} %q_hbm.1, ...), custom_call_target="tpu_custom_call" | custom-call | flops 3000000000 | bytes 8000000 | tf_op jit(solution)/shard_map/pallas_call | solution.py:399
  101.9 2.3 %copy.15 = bf16[128,4096]{1,0:T(8,128)(2,1)} copy(bf16[128,4096]{1,0:T(8,128)(2,1)} %shard_map.127) | data formatting | bytes 2097152
